TPU v7x, 32 devices: a whole 2x2x4 slice. The times are simulated.
32 devices in a mesh: dp: 4 (over z), bank: 4 (over y, x), head: 2 (over core).
Axes of the slice: x: 2, y: 2, z: 4, core: 2. Of those that a mesh axis runs over, the one named last changes fastest.
Arguments:
- feats: bfloat16 [2048, 2048], P('dp'), may hold values from -6 to 6
- w_first: bfloat16 [2048, 2048], P(None, ('bank', 'head')), may hold values from -0.125 to 0.125
- w_second: bfloat16 [2048, 256], P(('bank', 'head')), may hold values from -0.125 to 0.125
- fresh_keys: float32 [2048, 256], P('dp'), may hold values from -6 to 6
- bank: float32 [32768, 256], P(('bank', 'head'))
- block_lists: int32 [4, 32], P('dp'), may hold values from 0 to 63, as said below
- dest_rows: int32 [2048], P('dp'), may hold values from 0 to 32767, as said below
Outputs:
- loss: float32 [2048], P('dp')
- grad_first: float32 [2048, 2048], P('dp', ('bank', 'head'))
- grad_second: float32 [2048, 256], P(('bank', 'head'))
- new_bank: float32 [32768, 256], P(('bank', 'head'))
Inputs may be any that keep to these rules, and one draw needn't show every extreme that they name: `block_lists`: each row names 32 different blocks. `dest_rows`: all entries differ; the 512 entries of query block g name exactly 64 rows in each range of rows o * 4096 to (o + 1) * 4096 - 1.
All inputs are finite; a program needn't handle non-finite values.
Results may differ from a plain program's by a relative error of at most 0.012.
Values sent between devices are 32-bit elements; how exact they have to be, the bound alone decides.
A program may use at most 128 MiB of HBM per device.

v0:
```python
import jax
import jax.numpy as jnp
from jax import lax
from jax.sharding import PartitionSpec as P

BLOCK = 512
sharpness_divisor = 0.2
epsilon = 1e-06
lowest = -1e30


def joined(array, axis, combine):
    everything = jax.tree.map(lambda part: lax.all_gather(part, axis), array)
    leading = jax.tree.map(lambda part: part[0], everything)

    def hop(k, so_far):
        return combine(so_far, jax.tree.map(lambda part: part[k], everything))

    return lax.fori_loop(1, lax.axis_size(axis), hop, leading)


def unit_rows(values):
    norms = jnp.sqrt(jnp.sum(values * values, axis=1, keepdims=True) + epsilon)
    return (values / norms, norms)


def exact_scores(anchor_matrix, bank_entries):
    return (
        lax.dot_general(
            anchor_matrix,
            bank_entries,
            (((1,), (1,)), ((), ())),
            precision=lax.Precision.HIGHEST,
            preferred_element_type=jnp.float32,
        )
        / sharpness_divisor
    )


def join_stats(first, second):
    best = jnp.maximum(first[0], second[0])
    partition_total = first[1] * jnp.exp(first[0] - best) + second[1] * jnp.exp(second[0] - best)
    return (best, partition_total)


def shards(feats, w_first, w_second, fresh_keys, bank, block_lists, dest_rows):
    owner = lax.axis_index(("bank", "head"))
    owner_rows = bank.shape[0]
    hidden = jnp.maximum(jnp.dot(feats, w_first, preferred_element_type=jnp.float32), 0.0).astype(
        jnp.bfloat16
    )
    partial_embed = jnp.dot(hidden, w_second, preferred_element_type=jnp.float32)
    embed = lax.psum(partial_embed, ("bank", "head"))
    anchor_matrix, norms = unit_rows(embed)
    unit_length_bank, unused = unit_rows(fresh_keys)
    matching_similarity = jnp.sum(anchor_matrix * unit_length_bank, axis=1) / sharpness_divisor
    listed = block_lists[0]
    blocks_here = owner_rows // BLOCK
    owned = listed // blocks_here == owner
    owned_count = jnp.sum(owned.astype(jnp.int32))
    order = jnp.argsort(jnp.where(owned, 0, 1).astype(jnp.int32), stable=True)
    local_blocks = listed[order] - owner * blocks_here
    row_count = anchor_matrix.shape[0]

    def block_keys(index):
        return lax.dynamic_slice_in_dim(bank, local_blocks[index] * BLOCK, BLOCK, 0)

    start_best = jnp.full((row_count,), lowest, jnp.float32)
    start_total = jnp.zeros((row_count,), jnp.float32)
    start_weighted = jnp.zeros((row_count, anchor_matrix.shape[1]), jnp.float32)

    def first_pass(index, carry):
        best, partition_total = carry
        similarity_matrix = exact_scores(anchor_matrix, block_keys(index))
        new_best = jnp.maximum(best, jnp.max(similarity_matrix, axis=1))
        partition_total = partition_total * jnp.exp(best - new_best) + jnp.sum(
            jnp.exp(similarity_matrix - new_best[:, None]), axis=1
        )
        return (new_best, partition_total)

    local_stats = lax.fori_loop(0, owned_count, first_pass, (start_best, start_total))
    neg_best, neg_total = joined(local_stats, ("bank", "head"), join_stats)
    best = jnp.maximum(neg_best, matching_similarity)
    positive_weight = jnp.exp(matching_similarity - best)
    partition_total = neg_total * jnp.exp(neg_best - best) + positive_weight

    def second_pass(index, probability_mixed_bank):
        bank_entries = block_keys(index)
        shares = (
            jnp.exp(exact_scores(anchor_matrix, bank_entries) - best[:, None])
            / partition_total[:, None]
        )
        return probability_mixed_bank + jnp.dot(
            shares,
            bank_entries,
            precision=lax.Precision.HIGHEST,
            preferred_element_type=jnp.float32,
        )

    local_weighted = lax.fori_loop(0, owned_count, second_pass, start_weighted)
    probability_mixed_bank = lax.psum(local_weighted, ("bank", "head"))
    loss = best + jnp.log(partition_total) - matching_similarity
    anchor_derivative = (
        probability_mixed_bank
        + (positive_weight / partition_total - 1.0)[:, None] * unit_length_bank
    ) / sharpness_divisor
    inner = jnp.sum(anchor_matrix * anchor_derivative, axis=1, keepdims=True)
    grad_z = ((anchor_derivative - anchor_matrix * inner) / norms).astype(jnp.bfloat16)
    second_part = lax.dot_general(
        hidden, grad_z, (((0,), (0,)), ((), ())), preferred_element_type=jnp.float32
    )
    grad_second = lax.psum(second_part, "dp")
    grad_hidden = lax.dot_general(
        grad_z, w_second, (((1,), (1,)), ((), ())), preferred_element_type=jnp.float32
    )
    grad_pre = jnp.where(hidden > 0, grad_hidden, 0.0).astype(jnp.bfloat16)
    grad_first = lax.psum_scatter(
        lax.dot_general(
            feats, grad_pre, (((0,), (0,)), ((), ())), preferred_element_type=jnp.float32
        ),
        "dp",
        scatter_dimension=0,
        tiled=True,
    )
    got_keys, got_dest = (
        lax.all_gather(unit_length_bank, "dp", axis=0, tiled=True),
        lax.all_gather(dest_rows.astype(jnp.float32), "dp", axis=0, tiled=True),
    )
    local_rows = got_dest.astype(jnp.int32) - owner * owner_rows
    inside = (local_rows >= 0) & (local_rows < owner_rows)
    new_bank = bank.at[jnp.where(inside, local_rows, owner_rows)].set(got_keys, mode="drop")
    return (loss, grad_first, grad_second, new_bank)


def solution(mesh):
    return jax.shard_map(
        shards,
        mesh=mesh,
        in_specs=(
            P("dp", None),
            P(None, ("bank", "head")),
            P(("bank", "head"), None),
            P("dp", None),
            P(("bank", "head"), None),
            P("dp", None),
            P("dp"),
        ),
        out_specs=(
            P("dp"),
            P("dp", ("bank", "head")),
            P(("bank", "head"), None),
            P(("bank", "head"), None),
        ),
        check_vma=False,
    )
```

profile of v0, /device:TPU:0, one launch (start us, length us, event | category | flops | bytes accessed | tf_op | source)
XLA Modules:
  0.0 383.6 jit_solution(11246029741084995186)
XLA Ops:
  7.2 4.6 %copy.49 = f32[4096,256]{1,0:T(8,128)} copy(f32[4096,256]{1,0:T(8,128)} %param.17) | data formatting | bytes 8388608
  11.9 0.7 fusion.9
  12.8 1.0 fusion.18
  13.9 1.6 sort.17
  15.5 0.7 gather_fusion
  16.2 0.7 fusion.14
  17.1 54.1 %all-reduce.4.cloned.1.call-done = f32[512,256]{1,0:T(8,128)} async-done(((f32[512,256]{1,0:T(8,128)}), f32[512,256]{1,0:T(8,128)}) %all-reduce.4.cloned.1.call-update) | async-done | bytes 524304 | tf_op jit(solution)/shard_map/psum | solution.py:53
  71.2 1.2 multiply_reduce_fusion.3
  72.5 2.0 multiply_reduce_fusion.1
  74.5 36.0 %while.39 = (s32[]{:T(128)}, f32[512]{0:T(512)S(1)}, f32[512]{0:T(512)S(1)}, s32[]{:T(128)}, s32[32]{0:T(128)S(1)}, /*index=5*/f32[4096,256]{1,0:T(8,128)}, f32[...) while((s32[]{:T(128)}, f32[512]{0:T(512)S(1)}, ...), condition=%wide.region_7.8_spmd, body=%wide.region_4.0_spmd.sunk | while | flops 806355968 | bytes 3172573 | solution.py:81
  75.2 0.7 dynamic_slice.49
  76.6 2.1 fusion.40
  79.6 0.7 dynamic_slice.49
  81.0 2.1 fusion.40
  84.0 0.7 dynamic_slice.49
  85.4 2.1 fusion.40
  88.5 0.7 dynamic_slice.49
  89.8 2.1 fusion.40
  94.2 2.1 fusion.40
  98.7 2.1 fusion.40
  101.7 0.7 dynamic_slice.49
  103.1 2.1 fusion.40
  107.5 2.1 fusion.40
  110.5 7.4 %all-gather.2 = f32[8,1,512]{2,1,0:T(1,128)S(1)} all-gather(f32[1,1,512]{2,1,0:T(1,128)S(1)} %bitcast.49), channel_id=2, replica_groups=mesh['dp'=4,'bank'=4,'head'=2] {'bank','head'}, dimensions={0}, use_global_device_ids=true | all-gather | bytes 18432 | tf_op jit(solution)/shard_map/all_gather | solution.py:13
  118.0 9.4 %all-gather.3 = f32[8,1,512]{2,1,0:T(1,128)S(1)} all-gather(f32[1,1,512]{2,1,0:T(1,128)S(1)} %bitcast.52), channel_id=3, replica_groups=mesh['dp'=4,'bank'=4,'head'=2] {'bank','head'}, dimensions={0}, use_global_device_ids=true | all-gather | bytes 18432 | tf_op jit(solution)/shard_map/all_gather | solution.py:13
  128.4 62.4 %while.41 = (s32[]{:T(128)}, f32[512,256]{1,0:T(8,128)S(1)}, s32[]{:T(128)}, s32[32]{0:T(128)}, f32[4096,256]{1,0:T(8,128)}, /*index=5*/f32[512,256]{1,0:T(8,128...) while((s32[]{:T(128)}, f32[512,256]{1,0:T(8,128)S(1)}, ...), condition=%wide.region_13.14_spmd, body=%wide.region_12.13_spmd.sunk | while | flops 1611530240 | bytes 4722921 | solution.py:100
  129.1 1.3 dynamic_slice.53
  130.9 2.2 fusion.45
  133.1 3.0 convolution_add_fusion.2
  136.8 1.3 dynamic_slice.53
  138.6 2.2 fusion.45
  140.8 3.0 convolution_add_fusion.2
  144.5 1.3 dynamic_slice.53
  146.3 2.2 fusion.45
  148.5 3.0 convolution_add_fusion.2
  152.2 1.3 dynamic_slice.53
  154.1 2.2 fusion.45
  156.3 3.0 convolution_add_fusion.2
  159.9 1.3 dynamic_slice.53
  161.8 2.2 fusion.45
  164.0 3.0 convolution_add_fusion.2
  167.7 1.3 dynamic_slice.53
  169.5 2.2 fusion.45
  171.7 3.0 convolution_add_fusion.2
  175.4 1.3 dynamic_slice.53
  177.2 2.2 fusion.45
  179.4 3.0 convolution_add_fusion.2
  183.1 1.3 dynamic_slice.53
  184.9 2.2 fusion.45
  187.1 3.0 convolution_add_fusion.2
  190.8 0.8 copy-done.2
  191.7 0.7 all-gather.7.cloned.1.call-update
  192.4 52.9 %all-reduce.6.cloned.1.call-done = f32[512,256]{1,0:T(8,128)} async-done(((f32[512,256]{1,0:T(8,128)}), f32[512,256]{1,0:T(8,128)}) %all-reduce.6.cloned.1.call-update) | async-done | bytes 524304 | tf_op jit(solution)/shard_map/psum | solution.py:101
  245.4 1.4 multiply_reduce_fusion
  246.8 2.0 divide_convert_fusion
  248.8 3.3 convolution_bitcast_fusion
  252.8 12.1 %all-gather.4 = f32[4,1,512]{2,1,0:T(1,128)S(1)} all-gather(f32[1,1,512]{2,1,0:T(1,128)S(1)} %bitcast.58), channel_id=1, replica_groups=mesh['dp'=4,'bank'=4,'head'=2] {'dp'}, dimensions={0}, use_global_device_ids=true | all-gather | bytes 10240 | tf_op jit(solution)/shard_map/all_gather | solution.py:127
  264.9 1.0 fusion.19
  265.9 27.0 %all-gather.7.cloned.1.call-done = f32[2048,256]{1,0:T(8,128)} async-done(((f32[512,256]{1,0:T(8,128)}), f32[2048,256]{1,0:T(8,128)}) %all-gather.7.cloned.1.call-update) | async-done | bytes 2097168 | tf_op jit(solution)/shard_map/all_gather | solution.py:126
  292.9 13.6 %scatter_fusion = f32[4096,256]{1,0:T(8,128)} fusion(f32[4096,256]{1,0:T(8,128)} %get-tuple-element.541, s32[2048]{0:T(1024)S(1)} %compare_select_fusion, f32[2048,256]{1,0:T(8,128)} %all-gather.7.cloned.1.call-done), kind=kCustom, calls=%fused_computation.1 | custom fusion | bytes 6299648 | tf_op jit(solution)/shard_map/scatter | solution.py:131
  306.5 31.3 %reduce-scatter.2.cloned.1.call-done = f32[512,256]{0,1:T(8,128)} async-done(((f32[2048,256]{0,1:T(8,128)}), f32[512,256]{0,1:T(8,128)}) %reduce-scatter.2.cloned.1.call-update) | async-done | bytes 524304 | tf_op jit(solution)/shard_map/reduce_scatter | solution.py:117
  337.9 2.0 copy.13
  339.9 35.6 %all-reduce.8.cloned.1.call-done = f32[256,256]{1,0:T(8,128)} async-done(((f32[256,256]{1,0:T(8,128)}), f32[256,256]{1,0:T(8,128)}) %all-reduce.8.cloned.1.call-update) | async-done | bytes 262160 | tf_op jit(solution)/shard_map/psum | solution.py:112
  375.4 1.7 copy.50
  (96 shorter events, 6.3 us)
Async XLA Ops:
  7.2 4.7 %copy-start = (bf16[512,2048]{1,0:T(8,128)(2,1)S(1)}, bf16[512,2048]{1,0:T(8,128)(2,1)}, u32[]{:S(2)}) copy-start(bf16[512,2048]{1,0:T(8,128)(2,1)} %param.13) | copy-start | bytes 6291460
  7.2 64.1 %all-reduce.4.cloned.1.call-start = ((), (), s32[]{:S(2)}) async-start(), calls=%async_computation.1 | async-start | bytes 1048576 | tf_op jit(solution)/shard_map/psum | solution.py:53
  7.2 4.6 %copy-start.9 = (bf16[2048,256]{1,0:T(8,128)(2,1)S(1)}, bf16[2048,256]{1,0:T(8,128)(2,1)}, u32[]{:S(2)}) copy-start(bf16[2048,256]{1,0:T(8,128)(2,1)} %param.14) | copy-start | bytes 3145732
  11.9 0.9 copy-start.6
  11.9 2.0 copy-start.1
  11.9 5.1 %copy-start.5 = (f32[512,256]{1,0:T(8,128)S(1)}, f32[512,256]{1,0:T(8,128)}, u32[]{:S(2)}) copy-start(f32[512,256]{1,0:T(8,128)} %param.16) | copy-start | bytes 1572868
  13.8 231.5 %all-reduce.6.cloned.1.call-start = ((), (), s32[]{:S(2)}) async-start(), calls=%async_computation.2 | async-start | bytes 1048576 | tf_op jit(solution)/shard_map/psum | solution.py:101
  110.5 17.2 %copy-start.8 = (s32[32]{0:T(128)}, s32[32]{0:T(128)S(1)}, u32[]{:S(2)}) copy-start(s32[32]{0:T(128)S(1)} %get-tuple-element.559) | copy-start | bytes 388
  190.8 0.8 copy-start.2
  191.6 55.2 %copy-start.3 = (f32[512,256]{1,0:T(8,128)S(1)}, f32[512,256]{1,0:T(8,128)}, u32[]{:S(2)}) copy-start(f32[512,256]{1,0:T(8,128)} %get-tuple-element.283) | copy-start | bytes 1572868
  191.6 101.3 %all-gather.7.cloned.1.call-start = ((), (), s32[]{:S(2)}) async-start(), calls=%async_computation.5 | async-start | bytes 2621440 | tf_op jit(solution)/shard_map/all_gather | solution.py:126
  192.4 145.5 %reduce-scatter.2.cloned.1.call-start = ((), (), s32[]{:S(2)}) async-start(), calls=%async_computation.3 | async-start | bytes 2621440 | tf_op jit(solution)/shard_map/reduce_scatter | solution.py:117
  252.1 0.7 copy-start.7
  252.1 12.8 %copy-start.4 = (bf16[512,256]{1,0:T(8,128)(2,1)S(1)}, bf16[512,256]{1,0:T(8,128)(2,1)}, u32[]{:S(2)}) copy-start(bf16[512,256]{1,0:T(8,128)(2,1)} %divide_convert_fusion) | copy-start | bytes 786436
  252.2 123.3 %all-reduce.8.cloned.1.call-start = ((), (), s32[]{:S(2)}) async-start(), calls=%async_computation.4 | async-start | bytes 524288 | tf_op jit(solution)/shard_map/psum | solution.py:112
Sparse Core Ops, SparseCore 0:
  13.9 57.2 all-reduce.3
  191.8 53.5 all-reduce.5
  247.5 45.3 all-gather.6
  295.1 42.7 reduce-scatter.1
  340.7 34.6 all-reduce.7
where the time goes:
time: 386 us; the launch traced here: 384 us
  waiting for transfers between devices  202 us (52%)
  matrix products  64.2 us (17%)
  local copies, waits for them, and re-layouts  39.8 us (10%)
  blocking collectives  28.9 us (7%)
  loops' own time  23.3 us (6%)
  between operations  14 us (4%)
  other arithmetic  11.7 us (3%)
    psum x1, waiting for transfers between devices, shards(): embed = lax.psum(partial_embed, ('bank', 'head'))  54.1 us
    psum x1, waiting for transfers between devices, shards(): probability_mixed_bank = lax.psum(local_weighted, ('bank', 'head'))  52.9 us
    psum x1, waiting for transfers between devices, shards(): grad_second = lax.psum(second_part, 'dp')  35.6 us
    dot_general x16, matrix products, exact_scores(): lax.dot_general(anchor_matrix, bank_entries, (((1,), (1,)), ((), ())), pr...  34.4 us
    reduce_scatter x1, waiting for transfers between devices, shards(): lax.psum_scatter(lax.dot_general(feats, grad_pre, (((0,), (0,)), ((), ())...  31.3 us
    all_gather x1, waiting for transfers between devices, shards(): lax.all_gather(unit_length_bank, 'dp', axis=0, tiled=True)  27 us
    dot_general x8, matrix products, second_pass(): jnp.dot(shares, bank_entries, precision=lax.Precision.HIGHEST, preferred_...  23.8 us
    all_gather x2, blocking collectives, joined(): everything = jax.tree.map(lambda part: lax.all_gather(part, axis), array)  16.8 us
  transfers between devices with their start and end apart: 5, of which 5 were waited for; matrix products, arithmetic and copies ran while one was open for 7% of the time, Pallas kernels for 0%

commit v1 on v0

--- a/solution.py
+++ b/solution.py
@@ -50,7 +50,7 @@
         jnp.bfloat16
     )
     partial_embed = jnp.dot(hidden, w_second, preferred_element_type=jnp.float32)
-    embed = lax.psum(partial_embed, ("bank", "head"))
+    embed = jnp.sum(lax.all_gather(partial_embed, ("bank", "head")), axis=0)
     anchor_matrix, norms = unit_rows(embed)
     unit_length_bank, unused = unit_rows(fresh_keys)
     matching_similarity = jnp.sum(anchor_matrix * unit_length_bank, axis=1) / sharpness_divisor

time: 386 us -> 368 us (0.953)
  waiting for transfers between devices: 202 us -> 184 us
    psum x1 -> x0, waiting for transfers between devices: 54.1 us -> none  [shards(): embed = lax.psum(partial_embed, ('bank', 'head'))]
    all_gather x0 -> x1, waiting for transfers between devices: none -> 36.3 us  [shards(): embed = jnp.sum(lax.all_gather(partial_embed, ('bank', 'head')), axis=0)]
where the time goes in v1:
time: 368 us; the launch traced here: 366 us
  waiting for transfers between devices  184 us (50%)
  matrix products  64.1 us (17%)
  local copies, waits for them, and re-layouts  39.8 us (11%)
  blocking collectives  28.9 us (8%)
  loops' own time  22 us (6%)
  between operations  14 us (4%)
  other arithmetic  13.1 us (4%)
    psum x1, waiting for transfers between devices, shards(): probability_mixed_bank = lax.psum(local_weighted, ('bank', 'head'))  53 us
    all_gather x1, waiting for transfers between devices, shards(): embed = jnp.sum(lax.all_gather(partial_embed, ('bank', 'head')), axis=0)  36.3 us
    psum x1, waiting for transfers between devices, shards(): grad_second = lax.psum(second_part, 'dp')  35.4 us
    dot_general x16, matrix products, exact_scores(): lax.dot_general(anchor_matrix, bank_entries, (((1,), (1,)), ((), ())), pr...  34.4 us
    reduce_scatter x1, waiting for transfers between devices, shards(): lax.psum_scatter(lax.dot_general(feats, grad_pre, (((0,), (0,)), ((), ())...  31.5 us
    all_gather x1, waiting for transfers between devices, shards(): lax.all_gather(unit_length_bank, 'dp', axis=0, tiled=True)  27 us
    dot_general x8, matrix products, second_pass(): jnp.dot(shares, bank_entries, precision=lax.Precision.HIGHEST, preferred_...  23.8 us
    all_gather x2, blocking collectives, joined(): everything = jax.tree.map(lambda part: lax.all_gather(part, axis), array)  16.8 us
  transfers between devices with their start and end apart: 5, of which 5 were waited for; matrix products, arithmetic and copies ran while one was open for 7% of the time, Pallas kernels for 0%

profile of v1, /device:TPU:0, one launch (start us, length us, event | category | flops | bytes accessed | tf_op | source)
XLA Modules:
  0.0 366.1 jit_solution(9619697608801127707)
XLA Ops:
  7.2 4.6 %copy.48 = f32[4096,256]{1,0:T(8,128)} copy(f32[4096,256]{1,0:T(8,128)} %param.17) | data formatting | bytes 8388608
  11.9 0.7 fusion.9
  12.8 1.0 fusion.18
  13.9 1.6 sort.17
  15.5 0.7 gather_fusion
  17.1 36.3 %all-gather.11.cloned.1.call-done = f32[4096,256]{1,0:T(8,128)} async-done(((f32[512,256]{1,0:T(8,128)}), f32[4096,256]{1,0:T(8,128)}) %all-gather.11.cloned.1.call-update) | async-done | bytes 4194320 | tf_op jit(solution)/shard_map/all_gather | solution.py:53
  53.4 2.5 reduce_sum.64
  56.1 2.0 multiply_reduce_fusion.1
  58.1 35.3 %while.39 = (s32[]{:T(128)}, f32[512]{0:T(512)S(1)}, f32[512]{0:T(512)S(1)}, s32[]{:T(128)}, s32[32]{0:T(128)S(1)}, /*index=5*/f32[4096,256]{1,0:T(8,128)}, f32[...) while((s32[]{:T(128)}, f32[512]{0:T(512)S(1)}, ...), condition=%wide.region_7.8_spmd, body=%wide.region_4.0_spmd.sunk | while | flops 806355968 | bytes 3172573 | solution.py:81
  58.8 0.7 dynamic_slice.49
  60.1 2.1 fusion.40
  63.1 0.7 dynamic_slice.49
  64.5 2.1 fusion.40
  67.5 0.7 dynamic_slice.49
  68.8 2.1 fusion.40
  71.8 0.7 dynamic_slice.49
  73.2 2.1 fusion.40
  76.1 0.7 dynamic_slice.49
  77.5 2.1 fusion.40
  80.5 0.7 dynamic_slice.49
  81.8 2.1 fusion.40
  86.2 2.1 fusion.40
  90.5 2.1 fusion.40
  93.5 7.4 %all-gather.3 = f32[8,1,512]{2,1,0:T(1,128)S(1)} all-gather(f32[1,1,512]{2,1,0:T(1,128)S(1)} %bitcast.51), channel_id=3, replica_groups=mesh['dp'=4,'bank'=4,'head'=2] {'bank','head'}, dimensions={0}, use_global_device_ids=true | all-gather | bytes 18432 | tf_op jit(solution)/shard_map/all_gather | solution.py:13
  100.9 9.4 %all-gather.4 = f32[8,1,512]{2,1,0:T(1,128)S(1)} all-gather(f32[1,1,512]{2,1,0:T(1,128)S(1)} %bitcast.54), channel_id=4, replica_groups=mesh['dp'=4,'bank'=4,'head'=2] {'bank','head'}, dimensions={0}, use_global_device_ids=true | all-gather | bytes 18432 | tf_op jit(solution)/shard_map/all_gather | solution.py:13
  111.3 61.8 %while.41 = (s32[]{:T(128)}, f32[512,256]{1,0:T(8,128)S(1)}, s32[]{:T(128)}, s32[32]{0:T(128)}, f32[4096,256]{1,0:T(8,128)}, /*index=5*/f32[512,256]{1,0:T(8,128...) while((s32[]{:T(128)}, f32[512,256]{1,0:T(8,128)S(1)}, ...), condition=%wide.region_13.14_spmd, body=%wide.region_12.13_spmd.sunk | while | flops 1611530240 | bytes 4722921 | solution.py:100
  112.0 1.3 dynamic_slice.53
  113.8 2.2 fusion.45
  116.0 3.0 convolution_add_fusion.2
  119.6 1.3 dynamic_slice.53
  121.4 2.2 fusion.45
  123.6 3.0 convolution_add_fusion.2
  127.3 1.3 dynamic_slice.53
  129.1 2.2 fusion.45
  131.3 3.0 convolution_add_fusion.2
  134.9 1.3 dynamic_slice.53
  136.7 2.2 fusion.45
  138.9 3.0 convolution_add_fusion.2
  142.5 1.3 dynamic_slice.53
  144.4 2.2 fusion.45
  146.6 3.0 convolution_add_fusion.2
  150.2 1.3 dynamic_slice.53
  152.0 2.2 fusion.45
  154.2 3.0 convolution_add_fusion.2
  157.8 1.3 dynamic_slice.53
  159.7 2.2 fusion.45
  161.9 3.0 convolution_add_fusion.2
  165.5 1.3 dynamic_slice.53
  167.3 2.2 fusion.45
  169.5 3.0 convolution_add_fusion.2
  173.1 0.8 copy-done.2
  174.0 0.7 all-gather.9.cloned.1.call-update
  174.7 53.0 %all-reduce.3.cloned.1.call-done = f32[512,256]{1,0:T(8,128)} async-done(((f32[512,256]{1,0:T(8,128)}), f32[512,256]{1,0:T(8,128)}) %all-reduce.3.cloned.1.call-update) | async-done | bytes 524304 | tf_op jit(solution)/shard_map/psum | solution.py:101
  227.8 1.4 multiply_reduce_fusion
  229.2 2.0 divide_convert_fusion
  231.2 3.3 convolution_bitcast_fusion
  235.2 12.1 %all-gather.5 = f32[4,1,512]{2,1,0:T(1,128)S(1)} all-gather(f32[1,1,512]{2,1,0:T(1,128)S(1)} %bitcast.60), channel_id=1, replica_groups=mesh['dp'=4,'bank'=4,'head'=2] {'dp'}, dimensions={0}, use_global_device_ids=true | all-gather | bytes 10240 | tf_op jit(solution)/shard_map/all_gather | solution.py:127
  247.4 1.0 fusion.19
  248.4 27.0 %all-gather.9.cloned.1.call-done = f32[2048,256]{1,0:T(8,128)} async-done(((f32[512,256]{1,0:T(8,128)}), f32[2048,256]{1,0:T(8,128)}) %all-gather.9.cloned.1.call-update) | async-done | bytes 2097168 | tf_op jit(solution)/shard_map/all_gather | solution.py:126
  275.4 13.6 %scatter_fusion = f32[4096,256]{1,0:T(8,128)} fusion(f32[4096,256]{1,0:T(8,128)} %get-tuple-element.541, s32[2048]{0:T(1024)S(1)} %compare_select_fusion, f32[2048,256]{1,0:T(8,128)} %all-gather.9.cloned.1.call-done), kind=kCustom, calls=%fused_computation.1 | custom fusion | bytes 6299648 | tf_op jit(solution)/shard_map/scatter | solution.py:131
  289.0 31.5 %reduce-scatter.2.cloned.1.call-done = f32[512,256]{0,1:T(8,128)} async-done(((f32[2048,256]{0,1:T(8,128)}), f32[512,256]{0,1:T(8,128)}) %reduce-scatter.2.cloned.1.call-update) | async-done | bytes 524304 | tf_op jit(solution)/shard_map/reduce_scatter | solution.py:117
  320.5 2.0 copy.13
  322.5 35.4 %all-reduce.5.cloned.1.call-done = f32[256,256]{1,0:T(8,128)} async-done(((f32[256,256]{1,0:T(8,128)}), f32[256,256]{1,0:T(8,128)}) %all-reduce.5.cloned.1.call-update) | async-done | bytes 262160 | tf_op jit(solution)/shard_map/psum | solution.py:112
  357.9 1.7 copy.49
  (97 shorter events, 6.4 us)
Async XLA Ops:
  7.2 4.7 %copy-start = (bf16[512,2048]{1,0:T(8,128)(2,1)S(1)}, bf16[512,2048]{1,0:T(8,128)(2,1)}, u32[]{:S(2)}) copy-start(bf16[512,2048]{1,0:T(8,128)(2,1)} %param.13) | copy-start | bytes 6291460
  7.2 46.2 %all-gather.11.cloned.1.call-start = ((), (), s32[]{:S(2)}) async-start(), calls=%async_computation.5 | async-start | bytes 4718592 | tf_op jit(solution)/shard_map/all_gather | solution.py:53
  7.2 4.6 %copy-start.9 = (bf16[2048,256]{1,0:T(8,128)(2,1)S(1)}, bf16[2048,256]{1,0:T(8,128)(2,1)}, u32[]{:S(2)}) copy-start(bf16[2048,256]{1,0:T(8,128)(2,1)} %param.14) | copy-start | bytes 3145732
  11.9 0.9 copy-start.6
  11.9 2.0 copy-start.1
  11.9 4.4 %copy-start.5 = (f32[512,256]{1,0:T(8,128)S(1)}, f32[512,256]{1,0:T(8,128)}, u32[]{:S(2)}) copy-start(f32[512,256]{1,0:T(8,128)} %param.16) | copy-start | bytes 1572868
  13.8 213.9 %all-reduce.3.cloned.1.call-start = ((), (), s32[]{:S(2)}) async-start(), calls=%async_computation.1 | async-start | bytes 1048576 | tf_op jit(solution)/shard_map/psum | solution.py:101
  93.5 17.2 %copy-start.8 = (s32[32]{0:T(128)}, s32[32]{0:T(128)S(1)}, u32[]{:S(2)}) copy-start(s32[32]{0:T(128)S(1)} %get-tuple-element.559) | copy-start | bytes 388
  173.1 0.8 copy-start.2
  173.9 55.3 %copy-start.3 = (f32[512,256]{1,0:T(8,128)S(1)}, f32[512,256]{1,0:T(8,128)}, u32[]{:S(2)}) copy-start(f32[512,256]{1,0:T(8,128)} %get-tuple-element.283) | copy-start | bytes 1572868
  173.9 101.4 %all-gather.9.cloned.1.call-start = ((), (), s32[]{:S(2)}) async-start(), calls=%async_computation.4 | async-start | bytes 2621440 | tf_op jit(solution)/shard_map/all_gather | solution.py:126
  174.7 145.8 %reduce-scatter.2.cloned.1.call-start = ((), (), s32[]{:S(2)}) async-start(), calls=%async_computation.2 | async-start | bytes 2621440 | tf_op jit(solution)/shard_map/reduce_scatter | solution.py:117
  234.5 0.7 copy-start.7
  234.5 12.8 %copy-start.4 = (bf16[512,256]{1,0:T(8,128)(2,1)S(1)}, bf16[512,256]{1,0:T(8,128)(2,1)}, u32[]{:S(2)}) copy-start(bf16[512,256]{1,0:T(8,128)(2,1)} %divide_convert_fusion) | copy-start | bytes 786436
  234.6 123.4 %all-reduce.5.cloned.1.call-start = ((), (), s32[]{:S(2)}) async-start(), calls=%async_computation.3 | async-start | bytes 524288 | tf_op jit(solution)/shard_map/psum | solution.py:112
Sparse Core Ops, SparseCore 0:
  13.9 39.4 all-gather.10
  174.1 53.6 all-reduce.2
  230.0 45.3 all-gather.8
  277.6 42.7 reduce-scatter.1
  323.2 34.6 all-reduce.4
